TPU v7x, 32 devices: a whole 2x2x4 slice. The times are simulated.
32 devices in a mesh: row: 8 (over y, x, core), col: 4 (over z).
Axes of the slice: x: 2, y: 2, z: 4, core: 2. Of those that a mesh axis runs over, the one named last changes fastest.
Arguments:
- amps: float32 [32, 4, 576, 576], P(None, None, 'row', 'col'), may hold values from -6 to 6
- integrals: float32 [4, 576, 32, 576], P(None, 'row', 'col'), may hold values from -0.5 to 0.5
- e_occ: float32 [32], replicated, may hold values from -2 to -0.5
- e_vir: float32 [576], replicated, may hold values from 0.5 to 3
Outputs:
- update: float32 [32, 32, 576, 576], P('row', 'col')
All inputs are finite; a program needn't handle non-finite values.
Results may differ from a plain program's by a relative error of at most 0.00007.
Values sent between devices are 32-bit elements; how exact they have to be, the bound alone decides.
A program may use at most 256 MiB of HBM per device.

v0:
```python
import jax
import jax.numpy as jnp
from jax import lax
from jax.sharding import PartitionSpec as P


def contract(left, right):
    return jnp.einsum(
        "ikac,kcjb->ijab",
        left,
        right,
        precision=lax.Precision.HIGHEST,
        preferred_element_type=jnp.float32,
    )


def shards(amps, integrals, e_occ, e_vir):
    row_count = lax.axis_size("row")
    col_count = lax.axis_size("col")
    row_index = lax.axis_index("row")
    col_index = lax.axis_index("col")
    occ_col = e_occ.shape[0] // col_count
    left = lax.all_to_all(amps, "row", split_axis=0, concat_axis=2, tiled=True)
    occ_row = e_occ.shape[0] // row_count
    i_energy = lax.dynamic_slice_in_dim(e_occ, row_index * occ_row, occ_row)
    j_energy = lax.dynamic_slice_in_dim(e_occ, col_index * occ_col, occ_col)
    gathered = lax.all_gather(integrals, "row", axis=1, tiled=True)
    contracted = contract(lax.all_gather(left, "col", axis=3, tiled=True), gathered)
    denom = (
        i_energy[:, None, None, None]
        + j_energy[None, :, None, None]
        - e_vir[None, None, :, None]
        - e_vir[None, None, None, :]
    )
    scaled = contracted / denom
    return scaled


def solution(mesh):
    placed = (P(None, None, "row", "col"), P(None, "row", "col", None), P(), P())
    return jax.shard_map(
        shards, mesh=mesh, in_specs=placed, out_specs=P("row", "col", None, None), check_vma=False
    )
```

profile of v0, /device:TPU:0, one launch (start us, length us, event | category | flops | bytes accessed | tf_op | source)
XLA Modules:
  0.0 1233.9 jit_solution(11959143219266197439)
XLA Ops:
  6.5 0.0 copy-start.1
  6.5 0.0 copy-start
  6.5 0.0 all-gather.5.cloned.1.call-start
  6.5 112.1 %all_to_all.18 = f32[32,4,72,144]{3,2,1,0:T(8,128)} all-to-all(f32[32,4,72,144]{3,2,1,0:T(8,128)} %param.4), channel_id=1, replica_groups=mesh['row'=8,'col'=4] {'row'}, dimensions={0} | all-to-all | bytes 10616832 | tf_op jit(solution)/shard_map/all_to_all | solution.py:23
  118.6 11.2 copy.6
  129.8 9.7 all_to_all.16
  139.5 0.0 all-gather.5.cloned.1.call-update
  139.5 0.0 all-gather.3.cloned.1.call-start
  139.6 6.4 copy.5
  146.0 0.0 all-gather.3.cloned.1.call-update
  146.0 0.0 copy-done.1
  146.0 0.1 dynamic_slice.7
  146.1 0.1 dynamic_slice.6
  146.2 0.1 broadcast_add_fusion
  146.3 0.0 copy-done
  146.3 0.1 broadcast_subtract_fusion
  146.3 393.0 %all-gather.5.cloned.1.call-done = f32[4,4,576,576]{2,3,1,0:T(8,128)} async-done(((f32[4,4,576,144]{2,3,1,0:T(8,128)}), f32[4,4,576,576]{2,3,1,0:T(8,128)}) %all-gather.5.cloned.1.call-update) | async-done | bytes 21233680 | tf_op jit(solution)/shard_map/all_gather | solution.py:28
  539.3 219.0 %all-gather.3.cloned.1.call-done = f32[4,576,8,576]{3,1,0,2:T(8,128)} async-done(((f32[4,72,8,576]{3,1,0,2:T(8,128)}), f32[4,576,8,576]{3,1,0,2:T(8,128)}) %all-gather.3.cloned.1.call-update) | async-done | bytes 42467344 | tf_op jit(solution)/shard_map/all_gather | solution.py:27
  758.4 421.4 %bitcast_divide_fusion = f32[4,8,576,576]{2,3,0,1:T(8,128)} fusion(f32[576]{0:T(1024)S(1)} %copy-done, f32[4,8,576]{2,0,1:T(4,128)S(1)} %broadcast_subtract_fusion, f32[4,4,576,576]{2,3,1,0:T(8,128)} %all-gather.5.cloned.1.call-done, f32[4,576,8,576]{3,1,0,2:T(8,128)} %all-gather.3.cloned.1.call-done), kind=kOutput, calls=%fused_computation | convolution fusion | flops 293555404800 | bytes 106244352 | tf_op jit(solution)/shard_map/ikac,kcjb->ijab/dot_general | solution.py:8
  1179.7 47.3 %copy.7 = f32[4,8,576,576]{3,2,1,0:T(8,128)} copy(f32[4,8,576,576]{2,3,0,1:T(8,128)} %bitcast_divide_fusion) | data formatting | bytes 84934656 | tf_op jit(solution)/shard_map/div | solution.py:35
Async XLA Ops:
  6.5 139.5 %copy-start.1 = (f32[32]{0:T(128)S(1)}, f32[32]{0:T(128)}, u32[]{:S(2)}) copy-start(f32[32]{0:T(128)} %param.6) | copy-start | bytes 388
  6.5 139.7 %copy-start = (f32[576]{0:T(1024)S(1)}, f32[576]{0:T(1024)}, u32[]{:S(2)}) copy-start(f32[576]{0:T(1024)} %param.7) | copy-start | bytes 6916
  6.5 532.8 %all-gather.5.cloned.1.call-start = ((), (), s32[]{:S(2)}) async-start(), calls=%async_computation.2 | async-start | bytes 29491200 | tf_op jit(solution)/shard_map/all_gather | solution.py:28
  139.5 618.8 %all-gather.3.cloned.1.call-start = ((), (), s32[]{:S(2)}) async-start(), calls=%async_computation.1 | async-start | bytes 53084160 | tf_op jit(solution)/shard_map/all_gather | solution.py:27
Sparse Core Ops, SparseCore 0:
  139.7 399.6 all-gather.4
  541.2 217.0 all-gather.2
where the time goes:
time: 1240 us; the launch traced here: 1230 us
  waiting for transfers between devices  612 us (49%)
  matrix products  421 us (34%)
  blocking collectives  112 us (9%)
  local copies, waits for them, and re-layouts  74.8 us (6%)
  between operations  13.4 us (1%)
    dot_general x1, matrix products, contract(): jnp.einsum('ikac,kcjb->ijab', left, right, precision=lax.Precision.HIGHES...  421 us
    all_gather x1, waiting for transfers between devices, shards(): lax.all_gather(left, 'col', axis=3, tiled=True)  393 us
    all_gather x1, waiting for transfers between devices, shards(): gathered = lax.all_gather(integrals, 'row', axis=1, tiled=True)  219 us
    all_to_all x1, blocking collectives, shards(): left = lax.all_to_all(amps, 'row', split_axis=0, concat_axis=2, tiled=True)  112 us
    div x1, local copies, waits for them, and re-layouts, shards(): scaled = contracted / denom  47.3 us
  transfers between devices with their start and end apart: 2, of which 2 were waited for; matrix products, arithmetic and copies ran while one was open for 1% of the time, Pallas kernels for 0%

commit v1 on v0

v1 whole, which is shorter than its diff:
```python
import jax
import jax.numpy as jnp
from jax import lax
from jax.sharding import PartitionSpec as P


def contract(left, right):
    return jnp.einsum(
        "ikac,kcjb->ijab",
        left,
        right,
        precision=lax.Precision.HIGH,
        preferred_element_type=jnp.float32,
    )


def shards(amps, integrals, e_occ, e_vir):
    row_count = lax.axis_size("row")
    col_count = lax.axis_size("col")
    row_index = lax.axis_index("row")
    col_index = lax.axis_index("col")
    occ_col = e_occ.shape[0] // col_count
    occ_row = e_occ.shape[0] // row_count
    i_energy = lax.dynamic_slice_in_dim(e_occ, row_index * occ_row, occ_row)
    j_energy = lax.dynamic_slice_in_dim(e_occ, col_index * occ_col, occ_col)
    by_owner = amps.reshape((row_count, occ_row) + amps.shape[1:])

    def exchange(source, i):
        return lax.all_to_all(source[:, i], "row", split_axis=0, concat_axis=2, tiled=True)

    def widen(left):
        return lax.all_gather(left, "col", axis=3, tiled=True)

    first = exchange(by_owner, 0)
    first, by_owner = lax.optimization_barrier((first, by_owner))
    lefts = [first] + [exchange(by_owner, i) for i in range(1, occ_row)]
    whole = widen(first)
    whole, integrals = lax.optimization_barrier((whole, integrals))
    gathered = lax.all_gather(integrals, "row", axis=1, tiled=True)
    pair = e_vir[:, None] + e_vir[None, :]
    virtuals = e_vir.shape[0]
    out = jnp.zeros((occ_row, occ_col, virtuals, virtuals), jnp.float32)
    update = None
    for i in range(occ_row):
        later = None
        if i + 1 < occ_row:
            if update is None:
                left, gathered = lax.optimization_barrier((lefts[i + 1], gathered))
            else:
                left, update = lax.optimization_barrier((lefts[i + 1], update))
            later = widen(left)
        if update is not None:
            out = lax.dynamic_update_slice(out, update, (i - 1, 0, 0, 0))
        denom = (i_energy[i] + j_energy)[None, :, None, None] - pair[None, None]
        update = contract(whole, gathered) / denom
        whole = later
    return lax.dynamic_update_slice(out, update, (occ_row - 1, 0, 0, 0))


def solution(mesh):
    placed = (P(None, None, "row", "col"), P(None, "row", "col", None), P(), P())
    return jax.shard_map(
        shards, mesh=mesh, in_specs=placed, out_specs=P("row", "col", None, None), check_vma=False
    )
```

time: 1240 us -> 923 us (0.74)
  waiting for transfers between devices: 612 us -> 310 us
  matrix products: 421 us -> 255 us
  local copies, waits for them, and re-layouts: 74.8 us -> 205 us
    all_gather x1 -> x4, waiting for transfers between devices: 393 us -> 115 us  [widen(): return lax.all_gather(left, 'col', axis=3, tiled=True)]
    dot_general x1 -> x4, matrix products: 421 us -> 255 us  [contract(): jnp.einsum('ikac,kcjb->ijab', left, right, precision=lax.Precision.HIGH,...]
    dynamic_update_slice x0 -> x3, local copies, waits for them, and re-layouts: none -> 77.2 us  [the longest x1 47.3 us: shards(): return lax.dynamic_update_slice(out, update, (occ_row - 1, 0, 0, 0))]
    optimization_barrier x0 -> x5, local copies, waits for them, and re-layouts: none -> 64.1 us  [the longest x2 59 us: shards(): left, gathered = lax.optimization_barrier((lefts[i + 1], gathered))]
    all_gather x1, waiting for transfers between devices: 219 us -> 171 us  [shards(): gathered = lax.all_gather(integrals, 'row', axis=1, tiled=True)]
    div x1 -> x0, local copies, waits for them, and re-layouts: 47.3 us -> none  [shards(): scaled = contracted / denom]
    all_gather x0 -> x3, local copies, waits for them, and re-layouts: none -> 26.5 us  [widen(): return lax.all_gather(left, 'col', axis=3, tiled=True)]
    all_to_all x0 -> x1, waiting for transfers between devices: none -> 24.2 us  [exchange(): lax.all_to_all(source[:, i], 'row', split_axis=0, concat_axis=2, tiled=True)]
  transfers between devices with their start and end apart: 2 -> 6, of which waited for: 2 -> 4; matrix products, arithmetic and copies ran while one was open for 1% -> 36% of each run, Pallas kernels for 0% -> 0%
where the time goes in v1:
time: 923 us; the launch traced here: 914 us
  waiting for transfers between devices  310 us (34%)
  matrix products  255 us (28%)
  local copies, waits for them, and re-layouts  205 us (22%)
  blocking collectives  121 us (13%)
  between operations  13.7 us (1%)
    dot_general x4, matrix products, contract(): jnp.einsum('ikac,kcjb->ijab', left, right, precision=lax.Precision.HIGH,...  255 us
    all_gather x1, waiting for transfers between devices, shards(): gathered = lax.all_gather(integrals, 'row', axis=1, tiled=True)  171 us
    all_to_all x3, blocking collectives, exchange(): lax.all_to_all(source[:, i], 'row', split_axis=0, concat_axis=2, tiled=True)  121 us
    all_gather x4, waiting for transfers between devices, widen(): return lax.all_gather(left, 'col', axis=3, tiled=True)  115 us
    optimization_barrier x2, local copies, waits for them, and re-layouts, shards(): left, gathered = lax.optimization_barrier((lefts[i + 1], gathered))  59 us
    dynamic_update_slice x1, local copies, waits for them, and re-layouts, shards(): return lax.dynamic_update_slice(out, update, (occ_row - 1, 0, 0, 0))  47.3 us
    dynamic_update_slice x2, local copies, waits for them, and re-layouts, shards(): out = lax.dynamic_update_slice(out, update, (i - 1, 0, 0, 0))  29.8 us
    all_gather x3, local copies, waits for them, and re-layouts, widen(): return lax.all_gather(left, 'col', axis=3, tiled=True)  26.5 us
  transfers between devices with their start and end apart: 6, of which 4 were waited for; matrix products, arithmetic and copies ran while one was open for 36% of the time, Pallas kernels for 0%

profile of v1, /device:TPU:0, one launch (start us, length us, event | category | flops | bytes accessed | tf_op | source)
XLA Modules:
  0.0 913.9 jit_solution(18220522464637636360)
XLA Ops:
  6.5 1.8 slice_bitcast_fusion
  8.4 34.4 %all_to_all.72 = f32[8,4,72,144]{3,2,1,0:T(8,128)S(1)} all-to-all(f32[8,4,72,144]{3,2,1,0:T(8,128)S(1)} %slice_bitcast_fusion), channel_id=1, replica_groups=mesh['row'=8,'col'=4] {'row'}, dimensions={0} | all-to-all | bytes 2654208 | tf_op jit(solution)/shard_map/all_to_all | solution.py:29
  42.7 2.2 copy.23
  44.9 2.1 all_to_all.55
  47.0 1.7 copy.26
  48.7 0.0 all-gather.6.cloned.1.call-update
  48.7 0.0 all-gather.8.cloned.1.call-start
  48.8 108.3 %all-gather.6.cloned.1.call-done = f32[1,4,576,576]{2,1,0,3:T(4,128)} async-done(((f32[1,4,576,144]{2,1,0,3:T(4,128)}), f32[1,4,576,576]{2,1,0,3:T(4,128)}) %all-gather.6.cloned.1.call-update) | async-done | bytes 5308432 | tf_op jit(solution)/shard_map/all_gather | solution.py:32
  157.1 0.0 all-gather.8.cloned.1.call-update
  157.1 0.0 all-gather.10.cloned.1.call-start
  157.2 5.1 slice_bitcast_fusion.1
  162.3 53.9 %all_to_all.73 = f32[8,4,72,144]{3,2,1,0:T(8,128)} all-to-all(f32[8,4,72,144]{3,2,1,0:T(8,128)S(1)} %get-tuple-element.28), channel_id=1, replica_groups=mesh['row'=8,'col'=4] {'row'}, dimensions={0} | all-to-all | bytes 2654208 | tf_op jit(solution)/shard_map/all_to_all | solution.py:29
  216.2 3.3 copy.25
  219.6 3.0 all_to_all.63
  222.6 170.9 %all-gather.8.cloned.1.call-done = f32[4,576,8,576]{3,2,1,0:T(8,128)} async-done(((f32[4,72,8,576]{3,2,1,0:T(8,128)}), f32[4,576,8,576]{3,2,1,0:T(8,128)}) %all-gather.8.cloned.1.call-update) | async-done | bytes 42467344 | tf_op jit(solution)/shard_map/all_gather | solution.py:39
  393.5 3.0 copy.30
  396.6 0.0 all-gather.10.cloned.1.call-update
  396.6 4.4 all-to-all-start.1
  401.0 0.0 all-gather.12.cloned.1.call-start
  401.0 0.1 dynamic_slice.6
  401.1 0.7 fusion.18
  401.8 1.3 broadcast_add_fusion.1
  403.1 1.8 broadcast_add_fusion.2
  404.9 1.3 broadcast_add_fusion
  406.2 24.2 %all-to-all-done.1 = f32[8,4,72,144]{3,2,1,0:T(8,128)} async-done(((f32[8,4,72,144]{3,2,1,0:T(8,128)}), f32[8,4,72,144]{3,2,1,0:T(8,128)}, u32[]{:S(2)}, u32[]{:S(2)}) %all-to-all-start.1) | async-done | bytes 1327136 | tf_op jit(solution)/shard_map/all_to_all | solution.py:29
  430.4 3.3 copy.24
  433.7 2.9 all_to_all.59
  436.7 8.8 copy.28
  445.5 55.9 %copy.27 = f32[4,576,8,576]{1,3,0,2:T(8,128)} copy(f32[4,576,8,576]{3,2,1,0:T(8,128)} %all-gather.8.cloned.1.call-done) | data formatting | bytes 84934656 | tf_op jit(solution)/shard_map/optimization_barrier | solution.py:48
  501.4 64.1 %bitcast_divide_fusion.3 = f32[1,8,576,576]{2,3,1,0:T(8,128)} fusion(f32[4,576,8,576]{1,3,0,2:T(8,128)} %copy.27, f32[4,576,576]{2,1,0:T(8,128)} %copy.28, f32[576,576]{0,1:T(8,128)} %broadcast_add_fusion, f32[8]{0:T(128)S(1)} %get-tuple-element.32), kind=kOutput, calls=%fused_computation.5 | convolution fusion | flops 36697079808 | bytes 59719712 | tf_op jit(solution)/shard_map/ikac,kcjb->ijab/dot_general | solution.py:8
  565.5 1.7 copy.33
  567.2 0.0 all-gather.12.cloned.1.call-update
  567.2 0.0 all-gather.14.cloned.1.call-start
  567.3 32.8 %all_to_all.74 = f32[8,4,72,144]{3,2,1,0:T(8,128)} all-to-all(f32[8,4,72,144]{3,2,1,0:T(8,128)S(1)} %get-tuple-element.27), channel_id=1, replica_groups=mesh['row'=8,'col'=4] {'row'}, dimensions={0} | all-to-all | bytes 2654208 | tf_op jit(solution)/shard_map/all_to_all | solution.py:29
  600.0 2.4 copy.29
  602.5 1.9 all_to_all.67
  604.4 8.9 copy.31
  613.3 63.9 %bitcast_divide_fusion.2 = f32[1,8,576,576]{2,3,1,0:T(8,128)} fusion(f32[4,576,8,576]{1,3,0,2:T(8,128)} %copy.27, f32[1,4,576,576]{3,2,1,0:T(8,128)} %copy.31, f32[8]{0:T(128)S(1)} %get-tuple-element.31, f32[576,576]{0,1:T(8,128)S(1)} %copy-done.3), kind=kOutput, calls=%fused_computation.4 | convolution fusion | flops 36697079808 | bytes 59719712 | tf_op jit(solution)/shard_map/ikac,kcjb->ijab/dot_general | solution.py:8
  677.2 1.7 copy.36
  678.9 0.0 all-gather.14.cloned.1.call-update
  679.0 20.1 %dynamic_update_slice.12 = f32[4,8,576,576]{2,3,1,0:T(8,128)} pad(f32[1,8,576,576]{2,3,1,0:T(8,128)} %bitcast_divide_fusion.3, f32[]{:T(128)} %constant.10.clone.1), padding=0_3x0_0x0_0x0_0 | pad | bytes 53084164 | tf_op jit(solution)/shard_map/dynamic_update_slice | solution.py:53
  699.0 8.8 copy.34
  707.8 9.8 %constant_dynamic-update-slice_fusion = f32[4,8,576,576]{2,3,1,0:T(8,128)} fusion(f32[4,8,576,576]{2,3,1,0:T(8,128)} %dynamic_update_slice.12, f32[1,8,576,576]{2,3,1,0:T(8,128)} %bitcast_divide_fusion.2), kind=kLoop, calls=%fused_computation.19 | loop fusion | bytes 23592960 | tf_op jit(solution)/shard_map/dynamic_update_slice | solution.py:53
  717.6 63.1 %fusion.1 = f32[4,8,576,576]{2,3,1,0:T(8,128)} fusion(f32[4,8,576,576]{2,3,1,0:T(8,128)} %constant_dynamic-update-slice_fusion, f32[4,576,8,576]{1,3,0,2:T(8,128)} %copy.27, f32[1,4,576,576]{3,2,1,0:T(8,128)S(1)} %copy-done, f32[8]{0:T(128)S(1)} %get-tuple-element.30, f32[576,576]{0,1:T(8,128)S(1)} %copy-done.3), kind=kOutput, calls=%fused_computation.3 | convolution fusion | flops 36697079808 | bytes 65617952 | tf_op jit(solution)/shard_map/ikac,kcjb->ijab/dot_general | solution.py:8
  780.7 6.3 all-gather.14.cloned.1.call-done
  787.0 8.8 copy.37
  795.8 63.8 %fusion = f32[4,8,576,576]{2,3,1,0:T(8,128)} fusion(f32[4,8,576,576]{2,3,1,0:T(8,128)} %fusion.1, f32[4,576,8,576]{1,3,0,2:T(8,128)} %copy.27, f32[1,4,576,576]{3,2,1,0:T(8,128)} %copy.37, f32[8]{0:T(128)S(1)} %copy-done.6, f32[576,576]{0,1:T(8,128)S(1)} %copy-done.3), kind=kOutput, calls=%fused_computation.1 | convolution fusion | flops 36697079808 | bytes 66207776 | tf_op jit(solution)/shard_map/ikac,kcjb->ijab/dot_general | solution.py:8
  859.6 47.3 %copy.39 = f32[4,8,576,576]{3,2,1,0:T(8,128)} copy(f32[4,8,576,576]{2,3,1,0:T(8,128)} %fusion) | data formatting | bytes 84934656 | tf_op jit(solution)/shard_map/dynamic_update_slice | solution.py:57
  (17 shorter events, 0.0 us)
Async XLA Ops:
  6.5 150.6 %all-gather.6.cloned.1.call-start = ((), (), s32[]{:S(2)}) async-start(), calls=%async_computation.4 | async-start | bytes 7372800 | tf_op jit(solution)/shard_map/all_gather | solution.py:32
  48.7 344.8 %all-gather.8.cloned.1.call-start = ((), (), s32[]{:S(2)}) async-start(), calls=%async_computation.5 | async-start | bytes 53084160 | tf_op jit(solution)/shard_map/all_gather | solution.py:39
  157.1 447.2 %all-gather.10.cloned.1.call-start = ((), (), s32[]{:S(2)}) async-start(), calls=%async_computation.6 | async-start | bytes 7372800 | tf_op jit(solution)/shard_map/all_gather | solution.py:32
  219.6 181.5 %copy-start.5 = (f32[32]{0:T(128)S(1)}, f32[32]{0:T(128)}, u32[]{:S(2)}) copy-start(f32[32]{0:T(128)} %param.6) | copy-start | bytes 388
  219.6 185.3 %copy-start.4 = (f32[576]{0:T(1024)S(1)}, f32[576]{0:T(1024)}, u32[]{:S(2)}) copy-start(f32[576]{0:T(1024)} %param.7) | copy-start | bytes 6916
  396.6 33.9 %all-to-all-start.1 = ((f32[8,4,72,144]{3,2,1,0:T(8,128)}), f32[8,4,72,144]{3,2,1,0:T(8,128)}, u32[]{:S(2)}, u32[]{:S(2)}) async-start(f32[8,4,72,144]{3,2,1,0:T(8,128)} %get-tuple-element.29), calls=%async_computation.1 | async-start | bytes 4718592 | tf_op jit(solution)/shard_map/all_to_all | solution.py:29
  401.0 298.0 %all-gather.12.cloned.1.call-start = ((), (), s32[]{:S(2)}) async-start(), calls=%async_computation.7 | async-start | bytes 7372800 | tf_op jit(solution)/shard_map/all_gather | solution.py:32
  501.4 64.1 %copy-start.2 = (f32[1,4,576,144]{2,3,1,0:T(8,128)S(1)}, f32[1,4,576,144]{2,3,1,0:T(8,128)}, u32[]{:S(2)}) copy-start(f32[1,4,576,144]{2,3,1,0:T(8,128)} %all_to_all.59) | copy-start | bytes 3981316
  567.2 219.8 %all-gather.14.cloned.1.call-start = ((), (), s32[]{:S(2)}) async-start(), calls=%async_computation.8 | async-start | bytes 7372800 | tf_op jit(solution)/shard_map/all_gather | solution.py:32
  604.4 8.9 copy-start.3
  613.3 63.9 %copy-start.1 = (f32[1,4,576,144]{2,3,1,0:T(8,128)S(1)}, f32[1,4,576,144]{2,3,1,0:T(8,128)}, u32[]{:S(2)}) copy-start(f32[1,4,576,144]{2,3,1,0:T(8,128)} %all_to_all.67) | copy-start | bytes 3981316
  707.8 9.8 %copy-start = (f32[1,4,576,576]{3,2,1,0:T(8,128)S(1)}, f32[1,4,576,576]{3,2,1,0:T(8,128)}, u32[]{:S(2)}) copy-start(f32[1,4,576,576]{3,2,1,0:T(8,128)} %copy.34) | copy-start | bytes 15925252
  780.7 15.1 %copy-start.6 = (f32[8]{0:T(128)S(1)}, f32[8]{0:T(128)}, u32[]{:S(2)}) copy-start(f32[8]{0:T(128)} %get-tuple-element.25) | copy-start | bytes 100
Sparse Core Ops, SparseCore 0:
  48.8 108.2 all-gather.5
  159.0 234.4 all-gather.7
  396.7 108.8 all-gather.9
  567.3 108.0 all-gather.11
  679.1 107.9 all-gather.13
